TPU v7x, 32 devices: a whole 2x2x4 slice. The times are simulated.
32 devices in a mesh: rep: 16 (over z, x, core), fsdp: 2 (over y).
Axes of the slice: x: 2, y: 2, z: 4, core: 2. Of those that a mesh axis runs over, the one named last changes fastest.
Arguments:
- numerator: bfloat16 [16, 2560, 2560], P('rep', None, 'fsdp'), may hold values from -6 to 6
- push_weight: float32 [16], P('rep'), may hold values from 0.5 to 2
- norm_gain: float32 [2560], replicated, may hold values from 0.1 to 1.9
- activations: bfloat16 [2, 2816, 2560], P(None, ('rep', 'fsdp')), may hold values from -40 to 40, as said below
- cotangent: bfloat16 [2, 2816, 2560], P(None, ('rep', 'fsdp')), may hold values from -6 to 6
- step_index: int32 [], replicated, may hold values from 0 to 999
Outputs:
- mixed: bfloat16 [16, 2560, 2560], P('rep', None, 'fsdp')
- new_weight: float32 [16], P('rep')
Inputs may be any that keep to these rules, and one draw needn't show every extreme that they name: `activations`: Per-token and per-feature scales vary.
All inputs are finite; a program needn't handle non-finite values.
Results may differ from a plain program's by a relative error of at most 0.0075.
Values may be sent and summed in bfloat16 or wider, within the bound.
A program may use at most 128 MiB of HBM per device.

v0:
```python
from functools import partial

import jax
import jax.numpy as jnp
from jax import lax
from jax.experimental import pallas as pl
from jax.experimental.pallas import tpu as pltpu
from jax.sharding import PartitionSpec as P

LEARN_RATE = 1.5
EPSILON = 1e-05
PIECES = 4
CHUNK = 256
BLOCK = 512
ROWS = 16
PIECE = 48
MESH = pl.DeviceIdType.MESH


def shifted(block, axis, distance):
    count = lax.axis_size(axis)
    route = [((i - distance) % count, i) for i in range(count)]
    return lax.ppermute(block, axis, route)


def silu_slope(pre_act):
    sig = jax.nn.sigmoid(pre_act)
    return sig * (1.0 + pre_act * (1.0 - sig))


def normalised(activations, norm_gain):
    wide = activations.astype(jnp.float32)
    mean_square = jnp.mean(wide * wide, axis=-1, keepdims=True)
    return (wide * lax.rsqrt(mean_square + EPSILON) * norm_gain).astype(jnp.bfloat16)


def token_rows(activations, cotangent):
    count = lax.axis_size("fsdp")
    me = lax.axis_index("fsdp")
    width = cotangent.shape[2] // count
    acts, cots = [activations], [lax.dynamic_slice_in_dim(cotangent, me * width, width, 2)]
    for step in range(1, count):
        acts.append(shifted(activations, "fsdp", step))
        theirs = lax.rem(me + step, count)
        cots.append(shifted(lax.dynamic_slice_in_dim(cotangent, theirs * width, width, 2), "fsdp", step))
    return jnp.concatenate(acts, axis=1), jnp.concatenate(cots, axis=1)


def mix(state, hop_size):
    numerator, push_weight, normed, grad_out = state
    depth = numerator.shape[0]
    scale = depth ** (-0.5)
    rows = depth // PIECES
    mixed = []
    partner_weight = shifted(push_weight, "rep", hop_size)
    for start in range(0, depth, rows):
        grad = scale * jnp.einsum(
            "td,th->dh", normed[:, start : start + rows], grad_out, preferred_element_type=jnp.float32
        )
        update = (LEARN_RATE * grad).astype(jnp.bfloat16).astype(jnp.float32)
        local = (numerator[start : start + rows].astype(jnp.float32) - update).astype(jnp.bfloat16)
        theirs = shifted(local, "rep", hop_size)
        mixed.append((0.5 * (local.astype(jnp.float32) + theirs.astype(jnp.float32))).astype(jnp.bfloat16))
    return jnp.concatenate(mixed, axis=0), 0.5 * (push_weight + partner_weight)


def on_device(numerator, push_weight, norm_gain, activations, cotangent, step_index):
    acts, cots = token_rows(activations, cotangent)
    depth, width = numerator.shape[1:]
    scale = depth ** (-0.5)
    normed = normalised(acts, norm_gain).reshape(-1, depth)
    cots = cots.reshape(-1, width)
    eff_weight = (numerator[0].astype(jnp.float32) / push_weight[0]).astype(jnp.bfloat16)
    pre_act = scale * jnp.dot(normed, eff_weight, preferred_element_type=jnp.float32)
    grad_out = (cots.astype(jnp.float32) * silu_slope(pre_act)).astype(jnp.bfloat16)
    bit_count = lax.axis_size("rep").bit_length() - 1
    branches = [partial(mix, hop_size=2**bit) for bit in range(bit_count)]
    mixed, new_weight = lax.switch(
        step_index % bit_count, branches, (numerator[0], push_weight, normed, grad_out)
    )
    return mixed[None], new_weight


def push_kernel(
    hop_size, weight_ref, gain_ref, numer_hbm, act_hbm, cot_hbm, mixed_hbm, new_weight_ref,
    act_v, cot_v, normed_v, pre_v, grad_v, local_v, theirs_v, weight_v,
    load_sem, act_sem, act_send, act_recv, cot_sem, cot_send, cot_recv,
    state_send, state_recv, weight_send, weight_recv, out_sem, go_sem,
):
    rep, col = lax.axis_index("rep"), lax.axis_index("fsdp")
    n_rep = lax.axis_size("rep")
    mate = (rep, 1 - col)
    target = (lax.rem(rep + hop_size, n_rep), col)
    source = (lax.rem(rep + n_rep - hop_size, n_rep), col)
    odd = lax.rem(rep, 2)
    sibling = (rep + 1 - 2 * odd, col)
    leads = odd == (1 if hop_size == 1 else 0)
    tokens, depth = act_hbm.shape
    chunks, _, chunk = local_v.shape
    blocks = depth // BLOCK
    width = chunks * chunk
    scale = depth ** (-0.5)
    pieces = [(first, min(PIECE, tokens - first)) for first in range(0, tokens, PIECE)]

    def columns_of(c):
        return pl.ds(pl.multiple_of(c * chunk, chunk), chunk)

    def block_of(k):
        return pl.ds(pl.multiple_of(k * BLOCK, BLOCK), BLOCK)

    def load(c):
        return pltpu.make_async_copy(numer_hbm.at[:, columns_of(c)], local_v.at[c], load_sem.at[c])

    def own_cot(c):
        columns = pl.ds(pl.multiple_of(col * width + c * chunk, chunk), chunk)
        return pltpu.make_async_copy(cot_hbm.at[:, columns], cot_v.at[0, c], cot_sem.at[c])

    def send_cot(c):
        columns = pl.ds(pl.multiple_of((1 - col) * width + c * chunk, chunk), chunk)
        return pltpu.make_async_remote_copy(
            src_ref=cot_hbm.at[:, columns], dst_ref=cot_v.at[1, c],
            send_sem=cot_send.at[c], recv_sem=cot_recv.at[c], device_id=mate, device_id_type=MESH,
        )

    def send_act(i):
        rows = pl.ds(*pieces[i])
        return pltpu.make_async_remote_copy(
            src_ref=act_hbm.at[rows], dst_ref=act_v.at[1, rows],
            send_sem=act_send.at[i], recv_sem=act_recv.at[i], device_id=mate, device_id_type=MESH,
        )

    def send_state(c, k):
        return pltpu.make_async_remote_copy(
            src_ref=local_v.at[c, block_of(k)], dst_ref=theirs_v.at[c, block_of(k)],
            send_sem=state_send.at[c, k], recv_sem=state_recv.at[c, k], device_id=target, device_id_type=MESH,
        )

    def store(c, k):
        return pltpu.make_async_copy(
            theirs_v.at[c, block_of(k)], mixed_hbm.at[block_of(k), columns_of(c)], out_sem.at[c, k]
        )

    def start_sends():
        for i in range(len(pieces)):
            send_act(i).start()
        send_cot(0).start()

    send_weight = pltpu.make_async_remote_copy(
        src_ref=weight_v.at[0], dst_ref=weight_v.at[1],
        send_sem=weight_send, recv_sem=weight_recv, device_id=target, device_id_type=MESH,
    )
    own_act = pltpu.make_async_copy(act_hbm, act_v.at[0], act_sem)

    barrier = pltpu.get_barrier_semaphore()
    for device in (mate, source, sibling):
        pl.semaphore_signal(barrier, inc=1, device_id=device, device_id_type=MESH)
    own_act.start()
    weight_v[0] = jnp.full(weight_v.shape[1:], weight_ref[0], jnp.float32)
    pl.semaphore_wait(barrier, 3)

    @pl.when(leads)
    def _():
        start_sends()

    send_weight.start()
    for c in range(chunks):
        own_cot(c).start()
        load(c).start()

    gain = gain_ref[...].reshape(1, depth)

    def normalise(side, first, count):
        @pl.loop(0, count // ROWS)
        def _(i):
            rows = pl.ds(pl.multiple_of(first + i * ROWS, ROWS), ROWS)
            wide = act_v[side, rows, :].astype(jnp.float32)
            mean_square = jnp.mean(wide * wide, axis=-1, keepdims=True)
            normed = wide * lax.rsqrt(mean_square + EPSILON) * gain
            normed_v[pl.ds(pl.multiple_of(side * tokens + first + i * ROWS, ROWS), ROWS), :] = normed.astype(jnp.bfloat16)

    inverse = 1.0 / weight_v[0, 0:1, :]

    def forward(c, rows):
        pre_v[rows, :] = jnp.zeros((rows.size, chunk), jnp.float32)

        @pl.loop(0, blocks)
        def _(k):
            eff_weight = (local_v[c, block_of(k), :].astype(jnp.float32) * inverse).astype(jnp.bfloat16)
            pre_v[rows, :] += jnp.dot(normed_v[rows, block_of(k)], eff_weight, preferred_element_type=jnp.float32)

    def slopes(c, side):
        rows = pl.ds(side * tokens, tokens)
        grad_v[rows, :] = (
            cot_v[side, c].astype(jnp.float32) * silu_slope(scale * pre_v[rows, :])
        ).astype(jnp.bfloat16)

    def backward(c):
        @pl.loop(0, blocks)
        def _(k):
            grad = lax.dot_general(
                normed_v[:, block_of(k)], grad_v[...], (((0,), (0,)), ((), ())), preferred_element_type=jnp.float32
            )
            update = (LEARN_RATE * (scale * grad)).astype(jnp.bfloat16).astype(jnp.float32)
            local_v[c, block_of(k), :] = (local_v[c, block_of(k), :].astype(jnp.float32) - update).astype(jnp.bfloat16)
            send_state(c, k).start()

    own_act.wait()
    normalise(0, 0, tokens)
    load(0).wait()
    forward(0, pl.ds(0, tokens))
    own_cot(0).wait()
    slopes(0, 0)

    @pl.when(jnp.logical_not(leads))
    def _():
        pl.semaphore_wait(go_sem, 1)
        start_sends()

    for i in range(len(pieces)):
        send_act(i).wait_recv()
        normalise(1, *pieces[i])
    forward(0, pl.ds(tokens, tokens))
    send_cot(0).wait_recv()
    slopes(0, 1)
    for c in range(1, chunks):
        send_cot(c).start()

    @pl.when(leads)
    def _():
        pl.semaphore_signal(go_sem, inc=1, device_id=sibling, device_id_type=MESH)

    backward(0)

    @pl.loop(1, chunks)
    def _(c):
        load(c).wait()
        forward(c, pl.ds(0, 2 * tokens))
        own_cot(c).wait()
        slopes(c, 0)
        send_cot(c).wait_recv()
        slopes(c, 1)
        backward(c)

    send_weight.wait_recv()
    new_weight_ref[0] = jnp.max(0.5 * (weight_v[0] + weight_v[1]))

    @pl.loop(0, chunks)
    def _(c):
        @pl.loop(0, blocks)
        def _(k):
            send_state(c, k).wait_recv()
            both = local_v[c, block_of(k), :].astype(jnp.float32) + theirs_v[c, block_of(k), :].astype(jnp.float32)
            theirs_v[c, block_of(k), :] = (0.5 * both).astype(jnp.bfloat16)
            store(c, k).start()

    for i in range(len(pieces)):
        send_act(i).wait_send()
    send_weight.wait_send()

    @pl.loop(0, chunks)
    def _(c):
        send_cot(c).wait_send()

        @pl.loop(0, blocks)
        def _(k):
            send_state(c, k).wait_send()
            store(c, k).wait()


def push(state, hop_size, collective_id):
    numerator, push_weight, norm_gain, activations, cotangent = state
    depth, width = numerator.shape
    tokens = activations.shape[0]
    chunks, blocks = width // CHUNK, depth // BLOCK
    vmem, hbm = pl.BlockSpec(memory_space=pltpu.VMEM), pl.BlockSpec(memory_space=pl.ANY)
    smem = pl.BlockSpec(memory_space=pltpu.SMEM)
    dma = pltpu.SemaphoreType.DMA
    arrivals = -(-tokens // PIECE)
    return pl.pallas_call(
        partial(push_kernel, hop_size),
        out_shape=(
            jax.ShapeDtypeStruct((depth, width), jnp.bfloat16),
            jax.ShapeDtypeStruct((1,), jnp.float32),
        ),
        in_specs=[smem, vmem, hbm, hbm, hbm],
        out_specs=(hbm, smem),
        scratch_shapes=[
            pltpu.VMEM((2, tokens, depth), jnp.bfloat16),
            pltpu.VMEM((2, chunks, tokens, CHUNK), jnp.bfloat16),
            pltpu.VMEM((2 * tokens, depth), jnp.bfloat16),
            pltpu.VMEM((2 * tokens, CHUNK), jnp.float32),
            pltpu.VMEM((2 * tokens, CHUNK), jnp.bfloat16),
            pltpu.VMEM((chunks, depth, CHUNK), jnp.bfloat16),
            pltpu.VMEM((chunks, depth, CHUNK), jnp.bfloat16),
            pltpu.VMEM((2, 8, CHUNK), jnp.float32),
            dma((chunks,)), dma, dma((arrivals,)), dma((arrivals,)), dma((chunks,)), dma((chunks,)), dma((chunks,)),
            dma((chunks, blocks)), dma((chunks, blocks)), dma, dma, dma((chunks, blocks)),
            pltpu.SemaphoreType.REGULAR,
        ],
        compiler_params=pltpu.CompilerParams(
            collective_id=collective_id, has_side_effects=True, vmem_limit_bytes=48 * 2**20
        ),
        cost_estimate=pl.CostEstimate(
            flops=8 * tokens * depth * width, bytes_accessed=4 * depth * width, transcendentals=2 * tokens * width
        ),
    )(push_weight, norm_gain, numerator, activations, cotangent)


def on_pairs(numerator, push_weight, norm_gain, activations, cotangent, step_index):
    depth = numerator.shape[1]
    state = (
        numerator[0], push_weight, norm_gain,
        activations.reshape(-1, depth), cotangent.reshape(-1, cotangent.shape[2]),
    )
    bit_count = lax.axis_size("rep").bit_length() - 1
    branches = [partial(push, hop_size=2**bit, collective_id=bit) for bit in range(bit_count)]
    mixed, new_weight = lax.switch(step_index % bit_count, branches, state)
    return mixed[None], new_weight


def solution(mesh):
    placed = (
        P("rep", None, "fsdp"),
        P("rep"),
        P(),
        P(None, ("rep", "fsdp"), None),
        P(None, ("rep", "fsdp"), None),
        P(),
    )
    return jax.shard_map(
        on_pairs if mesh.shape["fsdp"] == 2 else on_device,
        mesh=mesh,
        in_specs=placed,
        out_specs=(P("rep", None, "fsdp"), P("rep")),
        check_vma=False,
    )
```

profile of v0, /device:TPU:1, one launch (start us, length us, event | category | flops | bytes accessed | tf_op | source)
XLA Modules:
  0.0 170.7 jit_solution(315107995930620194)
XLA Ops:
  1.3 164.8 %conditional.1 = (f32[1]{0:T(128)}, bf16[1,2560,1280]{2,1,0:T(8,128)(2,1)S(1)}) conditional(s32[]{:T(128)} %clamp.3, (f32[1]{0:T(128)}, f32[2560]{0:T(1024)}, bf16[2560,1280]{1,0:T(8,128)(2,1)}, bf16[176,2560]{1,0:T(8,128)(2,1)}, bf16[176,2560]{1,0:T(8,128)(2,1)}) %tuple.44, (f32[1]{0:T(128)}, f32[2560]{0:T(1024)}, ...), branch_computations={%region_0.1_spmd, %region_1.2_spmd, %region_2.3_spmd, %region_3.4_... | conditional | flops 4613734400 | bytes 13107216 | solution.py:317
  1.3 164.8 %branch_2_fun.1 = (bf16[2560,1280]{1,0:T(8,128)(2,1)S(1)}, f32[1]{0:T(128)}) custom-call(f32[1]{0:T(128)} %get-tuple-element.63.weight_ref, f32[2560]{0:T(1024)} %get-tuple-element.64.gain_ref, bf16[2560,1280]{1,0:T(8,128)(2,1)} %get-tuple-element.65.numer_hbm, bf16[176,2560]{1,0:T(8,128)(2,1)} %get-tuple-element.66.act_hbm, ...), custom_call_target="tpu_custom_call" | custom-call | flops 4613734400 | bytes 13107200 | tf_op jit(solution)/shard_map/cond/branch_2_fun/pallas_call | solution.py:279
  166.1 2.8 %copy.19 = bf16[1,2560,1280]{2,1,0:T(8,128)(2,1)} copy(bf16[1,2560,1280]{2,1,0:T(8,128)(2,1)S(1)} %get-tuple-element.93) | data formatting | bytes 13107200
where the time goes:
time: 171 us
  Pallas kernels  165 us (96%)
  between operations  3.11 us (2%)
  local copies, waits for them, and re-layouts  2.79 us (2%)
    pallas_call x1, Pallas kernels, push(): pl.pallas_call(partial(push_kernel, hop_size), out_shape=(jax.ShapeDtypeS...  165 us

commit v1 on v0

--- a/solution.py
+++ b/solution.py
@@ -83,7 +83,7 @@
 
 def push_kernel(
     hop_size, weight_ref, gain_ref, numer_hbm, act_hbm, cot_hbm, mixed_hbm, new_weight_ref,
-    act_v, cot_v, normed_v, pre_v, grad_v, local_v, theirs_v, weight_v,
+    act_v, cot_v, normed_v, turned_v, pre_v, grad_v, local_v, theirs_v, weight_v,
     load_sem, act_sem, act_send, act_recv, cot_sem, cot_send, cot_recv,
     state_send, state_recv, weight_send, weight_recv, out_sem, go_sem,
 ):
@@ -183,7 +183,7 @@
     def forward(c, rows):
         pre_v[rows, :] = jnp.zeros((rows.size, chunk), jnp.float32)
 
-        @pl.loop(0, blocks)
+        @pl.loop(0, blocks, unroll=True)
         def _(k):
             eff_weight = (local_v[c, block_of(k), :].astype(jnp.float32) * inverse).astype(jnp.bfloat16)
             pre_v[rows, :] += jnp.dot(normed_v[rows, block_of(k)], eff_weight, preferred_element_type=jnp.float32)
@@ -194,11 +194,20 @@
             cot_v[side, c].astype(jnp.float32) * silu_slope(scale * pre_v[rows, :])
         ).astype(jnp.bfloat16)
 
-    def backward(c):
-        @pl.loop(0, blocks)
+    def turn(side, k):
+        turned_v[side, block_of(k), :] = normed_v[pl.ds(side * tokens, tokens), block_of(k)].T
+
+    def backward(c, first=False):
+        @pl.loop(0, blocks, unroll=True)
         def _(k):
-            grad = lax.dot_general(
-                normed_v[:, block_of(k)], grad_v[...], (((0,), (0,)), ((), ())), preferred_element_type=jnp.float32
+            if first:
+                turn(1, k)
+            grad = sum(
+                jnp.dot(
+                    turned_v[side, block_of(k), :], grad_v[pl.ds(side * tokens, tokens), :],
+                    preferred_element_type=jnp.float32,
+                )
+                for side in range(2)
             )
             update = (LEARN_RATE * (scale * grad)).astype(jnp.bfloat16).astype(jnp.float32)
             local_v[c, block_of(k), :] = (local_v[c, block_of(k), :].astype(jnp.float32) - update).astype(jnp.bfloat16)
@@ -211,6 +220,10 @@
     own_cot(0).wait()
     slopes(0, 0)
 
+    @pl.loop(0, blocks)
+    def _(k):
+        turn(0, k)
+
     @pl.when(jnp.logical_not(leads))
     def _():
         pl.semaphore_wait(go_sem, 1)
@@ -219,17 +232,19 @@
     for i in range(len(pieces)):
         send_act(i).wait_recv()
         normalise(1, *pieces[i])
+        if i == len(pieces) - 2:
+
+            @pl.when(leads)
+            def _():
+                pl.semaphore_signal(go_sem, inc=1, device_id=sibling, device_id_type=MESH)
+
     forward(0, pl.ds(tokens, tokens))
     send_cot(0).wait_recv()
     slopes(0, 1)
     for c in range(1, chunks):
         send_cot(c).start()
 
-    @pl.when(leads)
-    def _():
-        pl.semaphore_signal(go_sem, inc=1, device_id=sibling, device_id_type=MESH)
-
-    backward(0)
+    backward(0, first=True)
 
     @pl.loop(1, chunks)
     def _(c):
@@ -288,6 +303,7 @@
             pltpu.VMEM((2, tokens, depth), jnp.bfloat16),
             pltpu.VMEM((2, chunks, tokens, CHUNK), jnp.bfloat16),
             pltpu.VMEM((2 * tokens, depth), jnp.bfloat16),
+            pltpu.VMEM((2, depth, tokens), jnp.bfloat16),
             pltpu.VMEM((2 * tokens, CHUNK), jnp.float32),
             pltpu.VMEM((2 * tokens, CHUNK), jnp.bfloat16),
             pltpu.VMEM((chunks, depth, CHUNK), jnp.bfloat16),

time: 171 us -> 313 us (1.83)
  Pallas kernels: 165 us -> 304 us
    pallas_call x1, Pallas kernels: 165 us -> 304 us  [push(): pl.pallas_call(partial(push_kernel, hop_size), out_shape=(jax.ShapeDtypeS...]
where the time goes in v1:
time: 313 us; the launch traced here: 310 us
  Pallas kernels  304 us (97%)
    pallas_call x1, Pallas kernels, push(): pl.pallas_call(partial(push_kernel, hop_size), out_shape=(jax.ShapeDtypeS...  304 us

profile of v1, /device:TPU:1, one launch (start us, length us, event | category | flops | bytes accessed | tf_op | source)
XLA Modules:
  0.0 310.2 jit_solution(23830654805425437)
XLA Ops:
  1.3 304.3 %conditional.1 = (f32[1]{0:T(128)}, bf16[1,2560,1280]{2,1,0:T(8,128)(2,1)S(1)}) conditional(s32[]{:T(128)} %clamp.3, (f32[1]{0:T(128)}, f32[2560]{0:T(1024)}, bf16[2560,1280]{1,0:T(8,128)(2,1)}, bf16[176,2560]{1,0:T(8,128)(2,1)}, bf16[176,2560]{1,0:T(8,128)(2,1)}) %tuple.44, (f32[1]{0:T(128)}, f32[2560]{0:T(1024)}, ...), branch_computations={%region_0.1_spmd, %region_1.2_spmd, %region_2.3_spmd, %region_3.4_... | conditional | flops 4613734400 | bytes 13107216 | solution.py:333
  1.6 303.8 %branch_3_fun.1 = (bf16[2560,1280]{1,0:T(8,128)(2,1)S(1)}, f32[1]{0:T(128)}) custom-call(f32[1]{0:T(128)} %get-tuple-element.70.weight_ref, f32[2560]{0:T(1024)} %get-tuple-element.71.gain_ref, bf16[2560,1280]{1,0:T(8,128)(2,1)} %get-tuple-element.72.numer_hbm, bf16[176,2560]{1,0:T(8,128)(2,1)} %get-tuple-element.73.act_hbm, ...), custom_call_target="tpu_custom_call" | custom-call | flops 4613734400 | bytes 13107200 | tf_op jit(solution)/shard_map/cond/branch_3_fun/pallas_call | solution.py:294
  305.6 2.8 copy.19

commit v2 on v1

--- a/solution.py
+++ b/solution.py
@@ -13,7 +13,8 @@
 CHUNK = 256
 BLOCK = 512
 ROWS = 16
-PIECE = 48
+LANES = 128
+SHARES = (64, 64, 32)
 MESH = pl.DeviceIdType.MESH
 
 
@@ -81,9 +82,18 @@
     return mixed[None], new_weight
 
 
+def pieces_of(tokens):
+    pieces, first = [], 0
+    for count in SHARES:
+        if first + count < tokens:
+            pieces.append((first, count))
+            first += count
+    return pieces + [(first, tokens - first)]
+
+
 def push_kernel(
     hop_size, weight_ref, gain_ref, numer_hbm, act_hbm, cot_hbm, mixed_hbm, new_weight_ref,
-    act_v, cot_v, normed_v, turned_v, pre_v, grad_v, local_v, theirs_v, weight_v,
+    act_v, cot_v, normed_v, turned_v, pre_v, grad_v, local_v, theirs_v, weight_v, eff_v,
     load_sem, act_sem, act_send, act_recv, cot_sem, cot_send, cot_recv,
     state_send, state_recv, weight_send, weight_recv, out_sem, go_sem,
 ):
@@ -100,7 +110,8 @@
     blocks = depth // BLOCK
     width = chunks * chunk
     scale = depth ** (-0.5)
-    pieces = [(first, min(PIECE, tokens - first)) for first in range(0, tokens, PIECE)]
+    pieces = pieces_of(tokens)
+    early = LANES if any(sum(piece) == LANES for piece in pieces[:-1]) else 0
 
     def columns_of(c):
         return pl.ds(pl.multiple_of(c * chunk, chunk), chunk)
@@ -155,6 +166,8 @@
     for device in (mate, source, sibling):
         pl.semaphore_signal(barrier, inc=1, device_id=device, device_id_type=MESH)
     own_act.start()
+    load(0).start()
+    own_cot(0).start()
     weight_v[0] = jnp.full(weight_v.shape[1:], weight_ref[0], jnp.float32)
     pl.semaphore_wait(barrier, 3)
 
@@ -163,7 +176,7 @@
         start_sends()
 
     send_weight.start()
-    for c in range(chunks):
+    for c in range(1, chunks):
         own_cot(c).start()
         load(c).start()
 
@@ -180,13 +193,14 @@
 
     inverse = 1.0 / weight_v[0, 0:1, :]
 
-    def forward(c, rows):
-        pre_v[rows, :] = jnp.zeros((rows.size, chunk), jnp.float32)
-
-        @pl.loop(0, blocks, unroll=True)
+    def weigh(c):
+        @pl.loop(0, blocks)
         def _(k):
-            eff_weight = (local_v[c, block_of(k), :].astype(jnp.float32) * inverse).astype(jnp.bfloat16)
-            pre_v[rows, :] += jnp.dot(normed_v[rows, block_of(k)], eff_weight, preferred_element_type=jnp.float32)
+            eff_v[block_of(k), :] = (local_v[c, block_of(k), :].astype(jnp.float32) * inverse).astype(jnp.bfloat16)
+
+    def forward(first, count):
+        rows = pl.ds(first, count)
+        pre_v[rows, :] = jnp.dot(normed_v[rows, :], eff_v[...], preferred_element_type=jnp.float32)
 
     def slopes(c, side):
         rows = pl.ds(side * tokens, tokens)
@@ -194,14 +208,14 @@
             cot_v[side, c].astype(jnp.float32) * silu_slope(scale * pre_v[rows, :])
         ).astype(jnp.bfloat16)
 
-    def turn(side, k):
-        turned_v[side, block_of(k), :] = normed_v[pl.ds(side * tokens, tokens), block_of(k)].T
+    def turn(side, k, first, count):
+        turned_v[side, block_of(k), pl.ds(first, count)] = normed_v[pl.ds(side * tokens + first, count), block_of(k)].T
 
     def backward(c, first=False):
         @pl.loop(0, blocks, unroll=True)
         def _(k):
             if first:
-                turn(1, k)
+                turn(1, k, early, tokens - early)
             grad = sum(
                 jnp.dot(
                     turned_v[side, block_of(k), :], grad_v[pl.ds(side * tokens, tokens), :],
@@ -216,13 +230,14 @@
     own_act.wait()
     normalise(0, 0, tokens)
     load(0).wait()
-    forward(0, pl.ds(0, tokens))
+    weigh(0)
+    forward(0, tokens)
     own_cot(0).wait()
     slopes(0, 0)
 
     @pl.loop(0, blocks)
     def _(k):
-        turn(0, k)
+        turn(0, k, 0, tokens)
 
     @pl.when(jnp.logical_not(leads))
     def _():
@@ -232,24 +247,30 @@
     for i in range(len(pieces)):
         send_act(i).wait_recv()
         normalise(1, *pieces[i])
-        if i == len(pieces) - 2:
-
-            @pl.when(leads)
-            def _():
-                pl.semaphore_signal(go_sem, inc=1, device_id=sibling, device_id_type=MESH)
-
-    forward(0, pl.ds(tokens, tokens))
+        forward(tokens + pieces[i][0], pieces[i][1])
+        if sum(pieces[i]) == early:
+
+            @pl.loop(0, blocks)
+            def _(k):
+                turn(1, k, 0, early)
+
     send_cot(0).wait_recv()
-    slopes(0, 1)
     for c in range(1, chunks):
         send_cot(c).start()
+
+    @pl.when(leads)
+    def _():
+        pl.semaphore_signal(go_sem, inc=1, device_id=sibling, device_id_type=MESH)
+
+    slopes(0, 1)
 
     backward(0, first=True)
 
     @pl.loop(1, chunks)
     def _(c):
         load(c).wait()
-        forward(c, pl.ds(0, 2 * tokens))
+        weigh(c)
+        forward(0, 2 * tokens)
         own_cot(c).wait()
         slopes(c, 0)
         send_cot(c).wait_recv()
@@ -290,7 +311,7 @@
     vmem, hbm = pl.BlockSpec(memory_space=pltpu.VMEM), pl.BlockSpec(memory_space=pl.ANY)
     smem = pl.BlockSpec(memory_space=pltpu.SMEM)
     dma = pltpu.SemaphoreType.DMA
-    arrivals = -(-tokens // PIECE)
+    arrivals = len(pieces_of(tokens))
     return pl.pallas_call(
         partial(push_kernel, hop_size),
         out_shape=(
@@ -309,6 +330,7 @@
             pltpu.VMEM((chunks, depth, CHUNK), jnp.bfloat16),
             pltpu.VMEM((chunks, depth, CHUNK), jnp.bfloat16),
             pltpu.VMEM((2, 8, CHUNK), jnp.float32),
+            pltpu.VMEM((depth, CHUNK), jnp.bfloat16),
             dma((chunks,)), dma, dma((arrivals,)), dma((arrivals,)), dma((chunks,)), dma((chunks,)), dma((chunks,)),
             dma((chunks, blocks)), dma((chunks, blocks)), dma, dma, dma((chunks, blocks)),
             pltpu.SemaphoreType.REGULAR,

time: 313 us -> 172 us (0.55)
  Pallas kernels: 304 us -> 165 us
    pallas_call x1, Pallas kernels: 304 us -> 165 us  [push(): pl.pallas_call(partial(push_kernel, hop_size), out_shape=(jax.ShapeDtypeS...]
where the time goes in v2:
time: 172 us
  Pallas kernels  165 us (96%)
  between operations  3.11 us (2%)
  local copies, waits for them, and re-layouts  2.79 us (2%)
    pallas_call x1, Pallas kernels, push(): pl.pallas_call(partial(push_kernel, hop_size), out_shape=(jax.ShapeDtypeS...  165 us

profile of v2, /device:TPU:1, one launch (start us, length us, event | category | flops | bytes accessed | tf_op | source)
XLA Modules:
  0.0 171.5 jit_solution(4422448002484774439)
XLA Ops:
  1.3 165.6 %conditional.1 = (f32[1]{0:T(128)}, bf16[1,2560,1280]{2,1,0:T(8,128)(2,1)S(1)}) conditional(s32[]{:T(128)} %clamp.3, (f32[1]{0:T(128)}, f32[2560]{0:T(1024)}, bf16[2560,1280]{1,0:T(8,128)(2,1)}, bf16[176,2560]{1,0:T(8,128)(2,1)}, bf16[176,2560]{1,0:T(8,128)(2,1)}) %tuple.44, (f32[1]{0:T(128)}, f32[2560]{0:T(1024)}, ...), branch_computations={%region_0.1_spmd, %region_1.2_spmd, %region_2.3_spmd, %region_3.4_... | conditional | flops 4613734400 | bytes 13107216 | solution.py:355
  1.3 165.4 %branch_1_fun.1 = (bf16[2560,1280]{1,0:T(8,128)(2,1)S(1)}, f32[1]{0:T(128)}) custom-call(f32[1]{0:T(128)} %get-tuple-element.56.weight_ref, f32[2560]{0:T(1024)} %get-tuple-element.57.gain_ref, bf16[2560,1280]{1,0:T(8,128)(2,1)} %get-tuple-element.58.numer_hbm, bf16[176,2560]{1,0:T(8,128)(2,1)} %get-tuple-element.59.act_hbm, ...), custom_call_target="tpu_custom_call" | custom-call | flops 4613734400 | bytes 13107200 | tf_op jit(solution)/shard_map/cond/branch_1_fun/pallas_call | solution.py:315
  166.9 2.8 %copy.19 = bf16[1,2560,1280]{2,1,0:T(8,128)(2,1)} copy(bf16[1,2560,1280]{2,1,0:T(8,128)(2,1)S(1)} %get-tuple-element.93) | data formatting | bytes 13107200
